TPU v7x, 256 devices: a whole 4x4x8 slice. The times are simulated.
256 devices in a mesh: tower: 8 (over x, core), peer: 32 (over z, y).
Axes of the slice: x: 4, y: 4, z: 8, core: 2. Of those that a mesh axis runs over, the one named last changes fastest.
Arguments:
- embeddings: bfloat16 [16384, 2048], P('tower', 'peer'), may hold values from -6 to 6
- session_lists: int32 [8, 2048], P('tower'), may hold values from 0 to 2047, each once within a row
- owners: int32 [16384, 1], P(('tower', 'peer')), may hold values from 0 to 7; in each aligned block of 64 rows (0 to 63, 64 to 127, ...) at most 16 rows name the same one
- counts: int32 [16384], P(('tower', 'peer')), may hold values from 1 to 3, as said below
- item_feats: bfloat16 [98304, 256], P(('tower', 'peer')), may hold values from -6 to 6
- cotangent: bfloat16 [98304, 1024], P(('tower', 'peer')), may hold values from -6 to 6
- cross_down: bfloat16 [2048, 256], replicated, may hold values from -0.125 to 0.125
- cross_up: bfloat16 [256, 2048], replicated, may hold values from -0.375 to 0.375
- compress: bfloat16 [2048, 256], replicated, may hold values from -0.125 to 0.125
- over_first: bfloat16 [512, 4096], replicated, may hold values from -0.25 to 0.25
- over_second: bfloat16 [4096, 1024], P('peer'), may hold values from -0.09375 to 0.09375
- over_third: bfloat16 [1024, 1024], replicated, may hold values from -0.1875 to 0.1875
Outputs:
- over_out: bfloat16 [98304, 1024], P(('tower', 'peer'))
- emb_grad: bfloat16 [16384, 2048], P('tower', 'peer')
Inputs may be any that keep to these rules, and one draw needn't show every extreme that they name: `session_lists`: each row is a permutation of the tower's 64 * 32 table rows. `owners`: within the 64 sessions of one device, no tower owns more than 16 of them. `counts`: the first session of every device has 3 samples and the second has one.
All inputs are finite; a program needn't handle non-finite values.
Results may differ from a plain program's by a relative error of at most 0.02.
Values may be sent and summed in bfloat16 or wider, within the bound.
A program may use at most 128 MiB of HBM per device.

v0:
```python
import jax
import jax.numpy as jnp
from jax import lax
from jax.sharding import PartitionSpec as P

MOSTC = 3


def silu_slope(pre):
    sigma = jax.nn.sigmoid(pre)
    return sigma * (1.0 + pre * (1.0 - sigma))


def times_t(left, right):
    return lax.dot_general(
        left, right, (((1,), (1,)), ((), ())), preferred_element_type=jnp.float32
    )


def body(
    embeddings,
    session_lists,
    owners,
    counts,
    item_feats,
    cotangent,
    cross_down,
    cross_up,
    compress,
    over_first,
    over_second,
    over_third,
):
    towers = lax.axis_size("tower")
    comp_width = compress.shape[1]
    grid_rows = item_feats.shape[0]
    slots = grid_rows // (towers * MOSTC)
    order = session_lists[0]
    picked = jnp.take(embeddings, order, axis=0)
    session_rows = lax.all_to_all(picked, "peer", split_axis=0, concat_axis=1, tiled=True)
    low = jnp.dot(session_rows, cross_down, preferred_element_type=jnp.float32).astype(jnp.bfloat16)
    lift = jnp.dot(low, cross_up, preferred_element_type=jnp.float32)
    rows_wide = session_rows.astype(jnp.float32)
    crossed = (rows_wide * lift + rows_wide).astype(jnp.bfloat16)
    compressed = jnp.dot(crossed, compress, preferred_element_type=jnp.float32).astype(jnp.bfloat16)
    owner_list = owners[:, 0]
    choose = (owner_list[:, None] == jnp.arange(towers, dtype=jnp.int32)[None, :]).astype(jnp.int32)
    earlier = jnp.cumsum(choose, axis=0) - choose
    position = jnp.sum(choose * earlier, axis=1)
    target = owner_list * slots + position
    dispatch = (target[:, None] == jnp.arange(towers * slots, dtype=jnp.int32)[None, :]).astype(
        jnp.int32
    )
    dispatch_half = dispatch.astype(jnp.bfloat16)
    send_rows = lax.dot_general(
        dispatch_half, compressed, (((0,), (0,)), ((), ())), preferred_element_type=jnp.float32
    ).astype(jnp.bfloat16)
    send_counts = jnp.sum(dispatch * counts[:, None], axis=0)
    repeated = jnp.broadcast_to(send_rows[:, None, :], (towers * slots, MOSTC, comp_width))
    repeated = repeated.reshape(towers, slots * MOSTC, comp_width)
    got_rows, got_counts = (
        lax.all_to_all(repeated, "tower", split_axis=0, concat_axis=0, tiled=True),
        lax.all_to_all(
            send_counts.reshape(towers, slots), "tower", split_axis=0, concat_axis=0, tiled=True
        ),
    )
    expanded = got_rows.reshape(grid_rows, comp_width)
    live = (
        jnp.arange(MOSTC, dtype=jnp.int32)[None, :] < got_counts.reshape(towers * slots)[:, None]
    ).astype(jnp.float32)
    live = live.reshape(grid_rows)
    inputs = jnp.concatenate([expanded, item_feats], axis=1)
    pre_first = jnp.dot(inputs, over_first, preferred_element_type=jnp.float32)
    hidden_first = jax.nn.silu(pre_first).astype(jnp.bfloat16)
    pre_second = jnp.dot(
        hidden_first,
        lax.all_gather(over_second, "peer", axis=0, tiled=True),
        preferred_element_type=jnp.float32,
    )
    hidden_second = jax.nn.silu(pre_second).astype(jnp.bfloat16)
    over_out = (
        jnp.dot(hidden_second, over_third, preferred_element_type=jnp.float32) * live[:, None]
    ).astype(jnp.bfloat16)
    masked = cotangent * live[:, None].astype(jnp.bfloat16)
    grad_second = (times_t(masked, over_third) * silu_slope(pre_second)).astype(jnp.bfloat16)
    back_first = times_t(grad_second, lax.all_gather(over_second, "peer", axis=0, tiled=True))
    grad_first = (back_first * silu_slope(pre_first)).astype(jnp.bfloat16)
    sample_grad = times_t(grad_first, over_first[:comp_width]).astype(jnp.bfloat16)
    returned = lax.all_to_all(
        sample_grad.reshape(towers, slots * MOSTC, comp_width),
        "tower",
        split_axis=0,
        concat_axis=0,
        tiled=True,
    )
    slot_grad = jnp.sum(
        returned.astype(jnp.float32).reshape(towers * slots, MOSTC, comp_width), axis=1
    ).astype(jnp.bfloat16)
    session_grad = jnp.dot(dispatch_half, slot_grad, preferred_element_type=jnp.float32).astype(
        jnp.bfloat16
    )
    grad_crossed = times_t(session_grad, compress).astype(jnp.bfloat16)
    grad_lift = (grad_crossed.astype(jnp.float32) * rows_wide).astype(jnp.bfloat16)
    grad_low = times_t(grad_lift, cross_up).astype(jnp.bfloat16)
    grad_rows = (
        grad_crossed.astype(jnp.float32) * (lift + 1.0) + times_t(grad_low, cross_down)
    ).astype(jnp.bfloat16)
    columns_back = lax.all_to_all(grad_rows, "peer", split_axis=1, concat_axis=0, tiled=True)
    emb_grad = jnp.zeros_like(embeddings).at[order].set(columns_back)
    return (over_out, emb_grad)


def solution(mesh):
    return jax.shard_map(
        body,
        mesh=mesh,
        in_specs=(
            P("tower", "peer"),
            P("tower", None),
            P(("tower", "peer"), None),
            P(("tower", "peer")),
            P(("tower", "peer"), None),
            P(("tower", "peer"), None),
            P(),
            P(),
            P(),
            P(),
            P("peer", None),
            P(),
        ),
        out_specs=(P(("tower", "peer"), None), P("tower", "peer")),
        check_vma=False,
    )
```

profile of v0, /device:TPU:32, one launch (start us, length us, event | category | flops | bytes accessed | tf_op | source)
XLA Modules:
  0.0 187.4 jit_solution(9144501375350728294)
XLA Ops:
  11.7 4.3 %all-to-all-start.2 = ((s32[8,1,16]{2,1,0:T(1,128)}), s32[8,1,16]{2,1,0:T(1,128)S(1)}, u32[]{:S(2)}, u32[]{:S(2)}) async-start(s32[8,1,16]{2,1,0:T(1,128)} %bitcast.8), calls=%async_computation.2 | async-start | bytes 8192 | tf_op jit(solution)/shard_map/all_to_all | solution.py:63
  16.0 1.2 copy.28
  17.7 1.3 reduce.7
  19.8 6.2 %gather_fusion = bf16[2048,64]{1,0:T(8,128)(2,1)S(1)} fusion(bf16[2048,64]{1,0:T(8,128)(2,1)S(1)} %copy.28, s32[2048]{0:T(1024)S(1)} %broadcast_clamp_fusion), kind=kCustom, calls=%fused_computation | custom fusion | bytes 532480 | tf_op jit(solution)/shard_map/jit(_take)/gather | solution.py:39
  27.4 11.4 %all-to-all-start = ((bf16[32,2,2048]{2,1,0:T(2,128)(2,1)}), bf16[32,2,2048]{2,1,0:T(2,128)(2,1)S(1)}, u32[]{:S(2)}, u32[]{:S(2)}) async-start(bf16[32,2,2048]{2,1,0:T(2,128)(2,1)} %reshape.142), calls=%async_computation | async-start | bytes 524288 | tf_op jit(solution)/shard_map/all_to_all | solution.py:40
  39.5 14.4 %all-to-all-done = bf16[32,2,2048]{2,1,0:T(2,128)(2,1)S(1)} async-done(((bf16[32,2,2048]{2,1,0:T(2,128)(2,1)}), bf16[32,2,2048]{2,1,0:T(2,128)(2,1)S(1)}, u32[]{:S(2)}, u32[]{:S(2)}) %all-to-all-start) | async-done | bytes 262176 | tf_op jit(solution)/shard_map/all_to_all | solution.py:40
  55.1 2.4 %fusion.8 = f32[64,2048]{1,0:T(8,128)S(1)} fusion(bf16[256,2048]{1,0:T(8,128)(2,1)} %param.19, bf16[64,2048]{1,0:T(8,128)(2,1)S(1)} %all_to_all.40, bf16[2048,256]{1,0:T(8,128)(2,1)} %param.18), kind=kOutput, calls=%fused_computation.22 | convolution fusion | flops 134234112 | bytes 2883584 | tf_op jit(solution)/shard_map/dot_general | solution.py:42
  57.5 1.7 convolution_convert_fusion.1
  60.1 4.5 %all-to-all-start.1 = ((bf16[8,48,256]{2,1,0:T(8,128)(2,1)}), bf16[8,48,256]{2,1,0:T(8,128)(2,1)S(1)}, u32[]{:S(2)}, u32[]{:S(2)}) async-start(bf16[8,48,256]{2,1,0:T(8,128)(2,1)} %reshape.102), calls=%async_computation.1 | async-start | bytes 393216 | tf_op jit(solution)/shard_map/all_to_all | solution.py:62
  64.9 6.5 %all-to-all-done.1 = bf16[8,48,256]{2,1,0:T(8,128)(2,1)S(1)} async-done(((bf16[8,48,256]{2,1,0:T(8,128)(2,1)}), bf16[8,48,256]{2,1,0:T(8,128)(2,1)S(1)}, u32[]{:S(2)}, u32[]{:S(2)}) %all-to-all-start.1) | async-done | bytes 196640 | tf_op jit(solution)/shard_map/all_to_all | solution.py:62
  71.4 6.7 %fusion.13 = f32[384,4096]{1,0:T(8,128)} fusion(bf16[512,4096]{1,0:T(8,128)(2,1)} %param.21, bf16[384,256]{1,0:T(8,128)(2,1)S(1)} %copy-done.1, bf16[384,256]{1,0:T(8,128)(2,1)S(1)} %bitcast.39), kind=kOutput, calls=%fused_computation.30 | convolution fusion | flops 1611399168 | bytes 10878976 | tf_op jit(solution)/shard_map/dot_general | solution.py:73
  78.1 34.4 %all-gather.2.cloned.1.call-done = bf16[4096,1024]{1,0:T(8,128)(2,1)} async-done(((bf16[128,1024]{1,0:T(8,128)(2,1)}), bf16[4096,1024]{1,0:T(8,128)(2,1)}) %all-gather.2.cloned.1.call-update) | async-done | bytes 8388624 | tf_op jit(solution)/shard_map/all_gather | solution.py:77
  112.5 8.1 %fusion = f32[384,1024]{1,0:T(8,128)S(1)} fusion(bf16[4096,1024]{1,0:T(8,128)(2,1)} %all-gather.2.cloned.1.call-done, f32[384,4096]{1,0:T(8,128)} %fusion.13), kind=kOutput, calls=%fused_computation.5 | convolution fusion | flops 3229089792 | bytes 16252928 | tf_op jit(solution)/shard_map/dot_general | solution.py:75
  120.7 1.2 copy-done.3
  121.8 2.1 %multiply_convert_fusion.3 = bf16[384,1024]{1,0:T(8,128)(2,1)} fusion(f32[384,1024]{1,0:T(8,128)S(1)} %fusion, bf16[1024,1024]{1,0:T(8,128)(2,1)S(1)} %copy-done, bf16[384,1024]{1,0:T(8,128)(2,1)S(1)} %copy-done.2, bf16[384]{0:T(512)(128)(2,1)S(1)} %convert_element_type.100), kind=kOutput, calls=%fused_computation.12 | convolution fusion | flops 809238528 | bytes 5243648 | tf_op jit(solution)/shard_map/dot_general | solution.py:15
  124.0 10.5 %fusion.5 = bf16[384,256]{1,0:T(8,128)(2,1)S(1)} fusion(bf16[512,4096]{1,0:T(8,128)(2,1)} %param.21, f32[384,4096]{1,0:T(8,128)} %fusion.13, bf16[384,1024]{1,0:T(8,128)(2,1)} %multiply_convert_fusion.3, bf16[4096,1024]{1,0:T(8,128)(2,1)} %all-gather.2.cloned.1.call-done), kind=kOutput, calls=%fused_computation.16 | convolution fusion | flops 4040785920 | bytes 17760256 | tf_op jit(solution)/shard_map/dot_general | solution.py:15
  134.5 10.9 %all_to_all.54 = bf16[8,48,256]{2,1,0:T(8,128)(2,1)S(1)} all-to-all(bf16[8,48,256]{2,1,0:T(8,128)(2,1)S(1)} %bitcast.41), channel_id=1, replica_groups=mesh['tower'=8,'peer'=32] {'tower'}, dimensions={0} | all-to-all | bytes 393216 | tf_op jit(solution)/shard_map/all_to_all | solution.py:89
  145.9 1.8 fusion.2
  147.6 3.5 %fusion.1 = bf16[64,2048]{1,0:T(8,128)(2,1)} fusion(bf16[2048,256]{1,0:T(8,128)(2,1)} %param.18, bf16[256,2048]{1,0:T(8,128)(2,1)} %param.19, f32[64,2048]{1,0:T(8,128)S(1)} %fusion.2, f32[64,2048]{1,0:T(8,128)S(1)} %fusion.8, bf16[64,2048]{1,0:T(8,128)(2,1)S(1)} %all_to_all.40), kind=kOutput, calls=%fused_computation.7 | convolution fusion | flops 135151616 | bytes 3670016 | tf_op jit(solution)/shard_map/dot_general | solution.py:15
  151.2 1.5 all_to_all.45
  153.9 7.6 %all-to-all-start.4 = ((bf16[32,2,2048]{2,1,0:T(2,128)(2,1)}), bf16[32,2,2048]{2,1,0:T(2,128)(2,1)S(1)}, u32[]{:S(2)}, u32[]{:S(2)}) async-start(bf16[32,2,2048]{2,1,0:T(2,128)(2,1)} %reshape.144), calls=%async_computation.4 | async-start | bytes 524288 | tf_op jit(solution)/shard_map/all_to_all | solution.py:108
  161.6 3.3 %multiply_convert_fusion.4 = bf16[384,1024]{1,0:T(8,128)(2,1)} fusion(bf16[1024,1024]{1,0:T(8,128)(2,1)S(1)} %copy-done, f32[384,1024]{1,0:T(8,128)} %copy-done.3, f32[384]{0:T(512)S(1)} %reshape.107), kind=kOutput, calls=%fused_computation.13 | convolution fusion | flops 808058880 | bytes 4457984 | tf_op jit(solution)/shard_map/dot_general | solution.py:82
  164.9 8.5 %all-to-all-done.4 = bf16[32,2,2048]{2,1,0:T(2,128)(2,1)S(1)} async-done(((bf16[32,2,2048]{2,1,0:T(2,128)(2,1)}), bf16[32,2,2048]{2,1,0:T(2,128)(2,1)S(1)}, u32[]{:S(2)}, u32[]{:S(2)}) %all-to-all-start.4) | async-done | bytes 262176 | tf_op jit(solution)/shard_map/all_to_all | solution.py:108
  173.8 5.9 %scatter_custom_fusion = bf16[2048,64]{1,0:T(8,128)(2,1)S(1)} fusion(s32[2048]{0:T(1024)S(1)} %bitcast.43, bf16[2048,64]{1,0:T(8,128)(2,1)S(1)} %bitcast.40, bf16[]{:T(256)} %constant.36.clone.1), kind=kCustom, calls=%fused_computation.35 | custom fusion | bytes 262146 | tf_op jit(solution)/shard_map/scatter | solution.py:109
  (39 shorter events, 13.2 us)
Async XLA Ops:
  7.2 114.7 %copy-start = (bf16[1024,1024]{1,0:T(8,128)(2,1)S(1)}, bf16[1024,1024]{1,0:T(8,128)(2,1)}, u32[]{:S(2)}) copy-start(bf16[1024,1024]{1,0:T(8,128)(2,1)} %param.23) | copy-start | bytes 6291460
  7.2 105.4 %all-gather.2.cloned.1.call-start = ((), (), s32[]{:S(2)}) async-start(), calls=%async_computation.5 | async-start | bytes 8650752 | tf_op jit(solution)/shard_map/all_gather | solution.py:77
  11.7 15.8 %all-to-all-start.2 = ((s32[8,1,16]{2,1,0:T(1,128)}), s32[8,1,16]{2,1,0:T(1,128)S(1)}, u32[]{:S(2)}, u32[]{:S(2)}) async-start(s32[8,1,16]{2,1,0:T(1,128)} %bitcast.8), calls=%async_computation.2 | async-start | bytes 8192 | tf_op jit(solution)/shard_map/all_to_all | solution.py:63
  27.4 26.5 %all-to-all-start = ((bf16[32,2,2048]{2,1,0:T(2,128)(2,1)}), bf16[32,2,2048]{2,1,0:T(2,128)(2,1)S(1)}, u32[]{:S(2)}, u32[]{:S(2)}) async-start(bf16[32,2,2048]{2,1,0:T(2,128)(2,1)} %reshape.142), calls=%async_computation | async-start | bytes 524288 | tf_op jit(solution)/shard_map/all_to_all | solution.py:40
  55.1 16.3 %copy-start.1 = (bf16[384,256]{1,0:T(8,128)(2,1)S(1)}, bf16[384,256]{1,0:T(8,128)(2,1)}, u32[]{:S(2)}) copy-start(bf16[384,256]{1,0:T(8,128)(2,1)} %param.16) | copy-start | bytes 589828
  60.1 11.3 %all-to-all-start.1 = ((bf16[8,48,256]{2,1,0:T(8,128)(2,1)}), bf16[8,48,256]{2,1,0:T(8,128)(2,1)S(1)}, u32[]{:S(2)}, u32[]{:S(2)}) async-start(bf16[8,48,256]{2,1,0:T(8,128)(2,1)} %reshape.102), calls=%async_computation.1 | async-start | bytes 393216 | tf_op jit(solution)/shard_map/all_to_all | solution.py:62
  112.5 9.3 %copy-start.2 = (bf16[384,1024]{1,0:T(8,128)(2,1)S(1)}, bf16[384,1024]{1,0:T(8,128)(2,1)}, u32[]{:S(2)}) copy-start(bf16[384,1024]{1,0:T(8,128)(2,1)} %param.17) | copy-start | bytes 2359300
  120.7 1.2 copy-start.3
  153.9 19.5 %all-to-all-start.4 = ((bf16[32,2,2048]{2,1,0:T(2,128)(2,1)}), bf16[32,2,2048]{2,1,0:T(2,128)(2,1)S(1)}, u32[]{:S(2)}, u32[]{:S(2)}) async-start(bf16[32,2,2048]{2,1,0:T(2,128)(2,1)} %reshape.144), calls=%async_computation.4 | async-start | bytes 524288 | tf_op jit(solution)/shard_map/all_to_all | solution.py:108
Sparse Core Ops, SparseCore 0:
  10.6 101.8 all-gather.1
where the time goes:
time: 188 us; the launch traced here: 187 us
  waiting for transfers between devices  64.6 us (34%)
  matrix products  40.1 us (21%)
  starting transfers between devices  27.8 us (15%)
  local copies, waits for them, and re-layouts  23.3 us (12%)
  between operations  14.2 us (8%)
  blocking collectives  10.9 us (6%)
  other arithmetic  6.42 us (3%)
    all_gather x1, waiting for transfers between devices, body(): lax.all_gather(over_second, 'peer', axis=0, tiled=True)  34.4 us
    dot_general x4, matrix products, times_t(): lax.dot_general(left, right, (((1,), (1,)), ((), ())), preferred_element_...  18 us
    all_to_all x1, waiting for transfers between devices, body(): lax.all_to_all(picked, 'peer', split_axis=0, concat_axis=1, tiled=True)  14.4 us
    all_to_all x1, starting transfers between devices, body(): lax.all_to_all(picked, 'peer', split_axis=0, concat_axis=1, tiled=True)  11.4 us
    all_to_all x1, blocking collectives, body(): lax.all_to_all(sample_grad.reshape(towers, slots * MOSTC, comp_width), 't...  10.9 us
    all_to_all x1, waiting for transfers between devices, body(): lax.all_to_all(grad_rows, 'peer', split_axis=1, concat_axis=0, tiled=True)  8.52 us
    dot_general x1, matrix products, body(): jnp.dot(hidden_first, lax.all_gather(over_second, 'peer', axis=0, tiled=T...  8.1 us
    all_to_all x1, starting transfers between devices, body(): lax.all_to_all(grad_rows, 'peer', split_axis=1, concat_axis=0, tiled=True)  7.63 us
  transfers between devices with their start and end apart: 5, of which 4 were waited for; matrix products, arithmetic and copies ran while one was open for 17% of the time, Pallas kernels for 0%

commit v1 on v0

--- a/solution.py
+++ b/solution.py
@@ -74,7 +74,9 @@
     hidden_first = jax.nn.silu(pre_first).astype(jnp.bfloat16)
     pre_second = jnp.dot(
         hidden_first,
-        lax.all_gather(over_second, "peer", axis=0, tiled=True),
+        jnp.concatenate(
+            lax.all_to_all(jnp.stack([over_second] * lax.axis_size("peer")), "peer", 0, 0), axis=0
+        ),
         preferred_element_type=jnp.float32,
     )
     hidden_second = jax.nn.silu(pre_second).astype(jnp.bfloat16)

time: 188 us -> 384 us (2.04)
  waiting for transfers between devices: 64.6 us -> 246 us
  blocking collectives: 10.9 us -> 20.9 us
  local copies, waits for them, and re-layouts: 23.3 us -> 27.8 us
    all_to_all x1, waiting for transfers between devices: 6.53 us -> 226 us  [body(): lax.all_to_all(jnp.stack([over_second] * lax.axis_size('peer')), 'peer',...]
    all_gather x1, waiting for transfers between devices: 34.4 us -> 0.01 us  [body(): lax.all_gather(over_second, 'peer', axis=0, tiled=True)]
    all_to_all x0 -> x1, blocking collectives: none -> 11.6 us  [body(): lax.all_to_all(repeated, 'tower', split_axis=0, concat_axis=0, tiled=True)]
    another operation x0 -> x1, local copies, waits for them, and re-layouts: none -> 4.29 us  [body(): jnp.stack([over_second] * lax.axis_size('peer'))]
  transfers between devices with their start and end apart: 5 -> 5, of which waited for: 4 -> 3; matrix products, arithmetic and copies ran while one was open for 17% -> 7% of each run, Pallas kernels for 0% -> 0%
where the time goes in v1:
time: 384 us; the launch traced here: 383 us
  waiting for transfers between devices  246 us (64%)
  matrix products  40.1 us (10%)
  starting transfers between devices  30.5 us (8%)
  local copies, waits for them, and re-layouts  27.8 us (7%)
  blocking collectives  20.9 us (5%)
  between operations  14.3 us (4%)
  other arithmetic  3.92 us (1%)
    all_to_all x1, waiting for transfers between devices, body(): lax.all_to_all(jnp.stack([over_second] * lax.axis_size('peer')), 'peer',...  226 us
    dot_general x4, matrix products, times_t(): lax.dot_general(left, right, (((1,), (1,)), ((), ())), preferred_element_...  18 us
    all_to_all x1, blocking collectives, body(): lax.all_to_all(repeated, 'tower', split_axis=0, concat_axis=0, tiled=True)  11.6 us
    all_to_all x1, starting transfers between devices, body(): lax.all_to_all(picked, 'peer', split_axis=0, concat_axis=1, tiled=True)  11.4 us
    all_to_all x1, waiting for transfers between devices, body(): lax.all_to_all(picked, 'peer', split_axis=0, concat_axis=1, tiled=True)  11 us
    all_to_all x1, blocking collectives, body(): lax.all_to_all(sample_grad.reshape(towers, slots * MOSTC, comp_width), 't...  9.23 us
    all_to_all x1, starting transfers between devices, body(): lax.all_to_all(grad_rows, 'peer', split_axis=1, concat_axis=0, tiled=True)  9.12 us
    all_to_all x1, waiting for transfers between devices, body(): lax.all_to_all(grad_rows, 'peer', split_axis=1, concat_axis=0, tiled=True)  8.53 us
  transfers between devices with their start and end apart: 5, of which 3 were waited for; matrix products, arithmetic and copies ran while one was open for 7% of the time, Pallas kernels for 0%

profile of v1, /device:TPU:32, one launch (start us, length us, event | category | flops | bytes accessed | tf_op | source)
XLA Modules:
  0.0 383.2 jit_solution(16028255149472484777)
XLA Ops:
  7.2 1.4 copy.28
  9.8 1.3 reduce.7
  11.3 6.2 %gather_fusion = bf16[2048,64]{1,0:T(8,128)(2,1)S(1)} fusion(bf16[2048,64]{1,0:T(8,128)(2,1)S(1)} %copy.28, s32[2048]{0:T(1024)S(1)} %broadcast_clamp_fusion), kind=kCustom, calls=%fused_computation | custom fusion | bytes 532480 | tf_op jit(solution)/shard_map/jit(_take)/gather | solution.py:39
  18.9 11.4 %all-to-all-start = ((bf16[32,2,2048]{2,1,0:T(2,128)(2,1)}), bf16[32,2,2048]{2,1,0:T(2,128)(2,1)S(1)}, u32[]{:S(2)}, u32[]{:S(2)}) async-start(bf16[32,2,2048]{2,1,0:T(2,128)(2,1)} %reshape.148), calls=%async_computation | async-start | bytes 524288 | tf_op jit(solution)/shard_map/all_to_all | solution.py:40
  31.4 11.0 %all-to-all-done = bf16[32,2,2048]{2,1,0:T(2,128)(2,1)S(1)} async-done(((bf16[32,2,2048]{2,1,0:T(2,128)(2,1)}), bf16[32,2,2048]{2,1,0:T(2,128)(2,1)S(1)}, u32[]{:S(2)}, u32[]{:S(2)}) %all-to-all-start) | async-done | bytes 262176 | tf_op jit(solution)/shard_map/all_to_all | solution.py:40
  42.4 4.3 %all-to-all-start.3 = ((s32[8,1,16]{2,1,0:T(1,128)}), s32[8,1,16]{2,1,0:T(1,128)S(1)}, u32[]{:S(2)}, u32[]{:S(2)}) async-start(s32[8,1,16]{2,1,0:T(1,128)} %bitcast.9), calls=%async_computation.3 | async-start | bytes 8192 | tf_op jit(solution)/shard_map/all_to_all | solution.py:63
  47.9 2.3 fusion.8
  50.2 1.7 convolution_convert_fusion.1
  52.9 11.6 %all_to_all.59 = bf16[8,48,256]{2,1,0:T(8,128)(2,1)S(1)} all-to-all(bf16[8,48,256]{2,1,0:T(8,128)(2,1)} %reshape.107), channel_id=1, replica_groups=mesh['tower'=8,'peer'=32] {'tower'}, dimensions={0} | all-to-all | bytes 393216 | tf_op jit(solution)/shard_map/all_to_all | solution.py:62
  64.5 4.3 %stack.2 = bf16[32,128,1024]{2,1,0:T(8,128)(2,1)} broadcast(bf16[128,1024]{1,0:T(8,128)(2,1)S(1)} %copy-done.1), dimensions={1,2} | broadcast | bytes 8650752 | tf_op jit(solution)/shard_map/stack | solution.py:78
  68.8 5.5 %all-to-all-start.2 = ((bf16[32,128,1024]{2,1,0:T(8,128)(2,1)}), bf16[32,128,1024]{2,1,0:T(8,128)(2,1)}, u32[]{:S(2)}, u32[]{:S(2)}) async-start(bf16[32,128,1024]{2,1,0:T(8,128)(2,1)} %stack.2), calls=%async_computation.2 | async-start | bytes 16777216 | tf_op jit(solution)/shard_map/all_to_all | solution.py:78
  76.0 6.7 %fusion.13 = f32[384,4096]{1,0:T(8,128)} fusion(bf16[512,4096]{1,0:T(8,128)(2,1)} %param.21, bf16[384,256]{1,0:T(8,128)(2,1)S(1)} %copy-done.2, bf16[384,256]{1,0:T(8,128)(2,1)S(1)} %bitcast.40), kind=kOutput, calls=%fused_computation.30 | convolution fusion | flops 1611399168 | bytes 10878976 | tf_op jit(solution)/shard_map/dot_general | solution.py:73
  82.7 225.7 %all-to-all-done.2 = bf16[32,128,1024]{2,1,0:T(8,128)(2,1)} async-done(((bf16[32,128,1024]{2,1,0:T(8,128)(2,1)}), bf16[32,128,1024]{2,1,0:T(8,128)(2,1)}, u32[]{:S(2)}, u32[]{:S(2)}) %all-to-all-start.2) | async-done | bytes 8388640 | tf_op jit(solution)/shard_map/all_to_all | solution.py:78
  308.4 8.1 %fusion = f32[384,1024]{1,0:T(8,128)S(1)} fusion(bf16[4096,1024]{1,0:T(8,128)(2,1)} %bitcast.8, f32[384,4096]{1,0:T(8,128)} %fusion.13), kind=kOutput, calls=%fused_computation.5 | convolution fusion | flops 3229089792 | bytes 16252928 | tf_op jit(solution)/shard_map/dot_general | solution.py:75
  317.8 2.1 multiply_convert_fusion.3
  320.0 10.5 %fusion.5 = bf16[384,256]{1,0:T(8,128)(2,1)S(1)} fusion(bf16[512,4096]{1,0:T(8,128)(2,1)} %param.21, f32[384,4096]{1,0:T(8,128)} %fusion.13, bf16[384,1024]{1,0:T(8,128)(2,1)} %multiply_convert_fusion.3, bf16[4096,1024]{1,0:T(8,128)(2,1)} %all-gather.2.cloned.1.call-done), kind=kOutput, calls=%fused_computation.16 | convolution fusion | flops 4040785920 | bytes 17760256 | tf_op jit(solution)/shard_map/dot_general | solution.py:15
  330.5 9.2 %all_to_all.60 = bf16[8,48,256]{2,1,0:T(8,128)(2,1)S(1)} all-to-all(bf16[8,48,256]{2,1,0:T(8,128)(2,1)S(1)} %bitcast.42), channel_id=1, replica_groups=mesh['tower'=8,'peer'=32] {'tower'}, dimensions={0} | all-to-all | bytes 393216 | tf_op jit(solution)/shard_map/all_to_all | solution.py:91
  340.2 1.8 fusion.2
  341.9 3.5 fusion.1
  345.5 1.5 all_to_all.49
  348.3 9.1 %all-to-all-start.5 = ((bf16[32,2,2048]{2,1,0:T(2,128)(2,1)}), bf16[32,2,2048]{2,1,0:T(2,128)(2,1)S(1)}, u32[]{:S(2)}, u32[]{:S(2)}) async-start(bf16[32,2,2048]{2,1,0:T(2,128)(2,1)} %reshape.150), calls=%async_computation.5 | async-start | bytes 524288 | tf_op jit(solution)/shard_map/all_to_all | solution.py:110
  357.4 3.3 multiply_convert_fusion.4
  360.7 8.5 %all-to-all-done.5 = bf16[32,2,2048]{2,1,0:T(2,128)(2,1)S(1)} async-done(((bf16[32,2,2048]{2,1,0:T(2,128)(2,1)}), bf16[32,2,2048]{2,1,0:T(2,128)(2,1)S(1)}, u32[]{:S(2)}, u32[]{:S(2)}) %all-to-all-start.5) | async-done | bytes 262176 | tf_op jit(solution)/shard_map/all_to_all | solution.py:110
  369.6 5.9 %scatter_custom_fusion = bf16[2048,64]{1,0:T(8,128)(2,1)S(1)} fusion(s32[2048]{0:T(1024)S(1)} %bitcast.44, bf16[2048,64]{1,0:T(8,128)(2,1)S(1)} %bitcast.41, bf16[]{:T(256)} %constant.36.clone.1), kind=kCustom, calls=%fused_computation.35 | custom fusion | bytes 262146 | tf_op jit(solution)/shard_map/scatter | solution.py:111
  (47 shorter events, 11.9 us)
Async XLA Ops:
  7.2 310.6 %copy-start = (bf16[1024,1024]{1,0:T(8,128)(2,1)S(1)}, bf16[1024,1024]{1,0:T(8,128)(2,1)}, u32[]{:S(2)}) copy-start(bf16[1024,1024]{1,0:T(8,128)(2,1)} %param.23) | copy-start | bytes 6291460
  7.2 23.1 %copy-start.3 = (s32[64,1]{0,1:T(1,128)S(1)}, s32[64,1]{0,1:T(1,128)}, u32[]{:S(2)}) copy-start(s32[64,1]{0,1:T(1,128)} %param.14) | copy-start | bytes 772
  7.2 23.4 %copy-start.5 = (s32[64]{0:T(128)S(1)}, s32[64]{0:T(128)}, u32[]{:S(2)}) copy-start(s32[64]{0:T(128)} %param.15) | copy-start | bytes 772
  18.9 23.5 %all-to-all-start = ((bf16[32,2,2048]{2,1,0:T(2,128)(2,1)}), bf16[32,2,2048]{2,1,0:T(2,128)(2,1)S(1)}, u32[]{:S(2)}, u32[]{:S(2)}) async-start(bf16[32,2,2048]{2,1,0:T(2,128)(2,1)} %reshape.148), calls=%async_computation | async-start | bytes 524288 | tf_op jit(solution)/shard_map/all_to_all | solution.py:40
  42.4 10.4 %all-to-all-start.3 = ((s32[8,1,16]{2,1,0:T(1,128)}), s32[8,1,16]{2,1,0:T(1,128)S(1)}, u32[]{:S(2)}, u32[]{:S(2)}) async-start(s32[8,1,16]{2,1,0:T(1,128)} %bitcast.9), calls=%async_computation.3 | async-start | bytes 8192 | tf_op jit(solution)/shard_map/all_to_all | solution.py:63
  46.7 17.8 %copy-start.1 = (bf16[128,1024]{1,0:T(8,128)(2,1)S(1)}, bf16[128,1024]{1,0:T(8,128)(2,1)}, u32[]{:S(2)}) copy-start(bf16[128,1024]{1,0:T(8,128)(2,1)} %param.22) | copy-start | bytes 786436
  68.8 7.2 %copy-start.2 = (bf16[384,256]{1,0:T(8,128)(2,1)S(1)}, bf16[384,256]{1,0:T(8,128)(2,1)}, u32[]{:S(2)}) copy-start(bf16[384,256]{1,0:T(8,128)(2,1)} %param.16) | copy-start | bytes 589828
  68.8 239.7 %all-to-all-start.2 = ((bf16[32,128,1024]{2,1,0:T(8,128)(2,1)}), bf16[32,128,1024]{2,1,0:T(8,128)(2,1)}, u32[]{:S(2)}, u32[]{:S(2)}) async-start(bf16[32,128,1024]{2,1,0:T(8,128)(2,1)} %stack.2), calls=%async_computation.2 | async-start | bytes 16777216 | tf_op jit(solution)/shard_map/all_to_all | solution.py:78
  74.3 245.7 %all-gather.2.cloned.1.call-start = ((), (), s32[]{:S(2)}) async-start(), calls=%async_computation.6 | async-start | bytes 8650752 | tf_op jit(solution)/shard_map/all_gather | solution.py:88
  308.4 9.4 %copy-start.4 = (bf16[384,1024]{1,0:T(8,128)(2,1)S(1)}, bf16[384,1024]{1,0:T(8,128)(2,1)}, u32[]{:S(2)}) copy-start(bf16[384,1024]{1,0:T(8,128)(2,1)} %param.17) | copy-start | bytes 2359300
  316.6 1.2 copy-start.6
  348.3 20.9 %all-to-all-start.5 = ((bf16[32,2,2048]{2,1,0:T(2,128)(2,1)}), bf16[32,2,2048]{2,1,0:T(2,128)(2,1)S(1)}, u32[]{:S(2)}, u32[]{:S(2)}) async-start(bf16[32,2,2048]{2,1,0:T(2,128)(2,1)} %reshape.150), calls=%async_computation.5 | async-start | bytes 524288 | tf_op jit(solution)/shard_map/all_to_all | solution.py:110
Sparse Core Ops, SparseCore 0:
  77.7 222.9 all-gather.1
